TPU v7x, 256 devices: a whole 4x4x8 slice. The times are simulated.
256 devices in a mesh: leaf: 64 (over z, x, core), dom: 4 (over y).
Axes of the slice: x: 4, y: 4, z: 8, core: 2. Of those that a mesh axis runs over, the one named last changes fastest.
Arguments:
- child_terms: float32 [1024, 64, 128], P(('leaf', 'dom')), may hold values from -0.5 to 0.5
- transfer: float32 [960, 64, 128], P('leaf')
- top_transfer: float32 [64, 64, 128], replicated
- coupling: float32 [65536, 64, 64], P(('leaf', 'dom')), may hold values from -6 to 6
- block_row: int32 [65536], P(('leaf', 'dom')), may hold values from 0 to 1023, as said below
- block_col: int32 [65536], P(('leaf', 'dom')), may hold values from 0 to 1023, as said below
Outputs:
- bottom_basis: float32 [1024, 64, 128], P(('leaf', 'dom'))
- local_basis: float32 [960, 64, 128], P('leaf')
- top_basis: float32 [64, 64, 128], P('leaf')
- root_factor: float32 [64, 64], replicated
- projected: float32 [65536, 64, 64], P(('leaf', 'dom'))
Inputs may be any that keep to these rules, and one draw needn't show every extreme that they name: block_row[b] // 16 == b // 1024. block_col[b] // 16 differs from block_row[b] // 16 by at most 3; both differences -3 and +3 occur.
All inputs are finite; a program needn't handle non-finite values.
Results may differ from a plain program's by a relative error of at most 0.0001.
Values sent between devices are 32-bit elements; how exact they have to be, the bound alone decides.
A program may use at most 128 MiB of HBM per device.

v0:
```python
import functools

import jax
import jax.numpy as jnp
from jax import lax
from jax.experimental import pallas as pl
from jax.experimental.pallas import tpu as pltpu
from jax.sharding import PartitionSpec as P

REACH = 3
K = 64
F32 = jnp.float32
BF = jnp.bfloat16
HIGH = lax.Precision.HIGHEST
MESH = pl.DeviceIdType.MESH
NN = ((1,), (0,))
NT = ((1,), (1,))


def dot(a, b, dims):
    return lax.dot_general(a, b, (dims, ((), ())), precision=HIGH, preferred_element_type=F32)


def dot16(a, b):
    return lax.dot_general(a, b, (NN, ((), ())), preferred_element_type=F32)


def split(x):
    high = x.astype(BF)
    return high, (x - high.astype(F32)).astype(BF)


def factor(grams, hook=None):
    count = len(grams)
    sub = lax.broadcasted_iota(jnp.int32, (1, 8, 128), 1)
    row = lax.broadcasted_iota(jnp.int32, (K, K), 0)
    col = lax.broadcasted_iota(jnp.int32, (K, K), 1)
    eye = jnp.where(row == col, 1.0, 0.0).astype(F32)
    rest = jnp.stack([jnp.concatenate([g, eye], axis=1) for g in grams])
    done = []
    for p in range(8):
        panel = rest[:, :8]
        rest = rest[:, 8:]
        left = 56 - 8 * p
        lanes = [8 * p + c for c in range(8)]
        cols = [jnp.broadcast_to(panel[:, :, c : c + 1], (count, 8, 128)) for c in lanes]
        below = [jnp.broadcast_to(rest[:, :, c : c + 1], (count, left, 128)) for c in lanes] if left else []
        out = jnp.zeros((count, 8, 128), F32)
        for k in range(8):
            here = sub == k
            pivot_row = jnp.broadcast_to(panel[:, k : k + 1, :], (count, 8, 128))
            heads = [jnp.broadcast_to(c[:, k : k + 1, :], (count, 8, 128)) for c in cols[k:]]
            out = jnp.where(here, pivot_row * lax.rsqrt(heads[0]), out)
            scale = jnp.where(here, -1.0, cols[k]) * (1.0 / heads[0])
            panel = jnp.where(here, 0.0, panel) - scale * pivot_row
            for c in range(k + 1, 8):
                cols[c] = jnp.where(here, 0.0, cols[c]) - scale * heads[c - k]
        done.append(out)
        for k in range(8 if left else 0):
            rest = rest - below[k] * jnp.broadcast_to(panel[:, k : k + 1, :], (count, left, 128))
        if hook is not None:
            hook(p)
    keep = lax.broadcasted_iota(jnp.int32, (K, 128), 1) >= lax.broadcasted_iota(jnp.int32, (K, 128), 0)
    return [jnp.where(keep, jnp.concatenate([d[n] for d in done], axis=0), 0.0) for n in range(count)]


def kernel(doms, leaves, child, transfer, toptr, coup, rows, cols,
           bottom_out, local_out, top_out, root_out, proj_out,
           win, ct, par, turned, us, lw, rw, xs, xr,
           in_sem, out_sem, gs, gr, ws, wr, bs, br, cs, cr, ds, dr, es, er):
    leaf = lax.axis_index("leaf")
    dom = lax.axis_index("dom")
    top_levels = leaves.bit_length() - 1
    dom_levels = doms.bit_length() - 1
    per = child.shape[0]
    nodes = per * doms
    half = nodes // 2
    last = (2 * REACH + 1) * nodes - 1

    coup_copy = pltpu.make_async_copy(coup, ct, in_sem.at[0])
    coup_copy.start()
    loads = [
        pltpu.make_async_copy(transfer.at[pl.ds(2 * dom, 2)], par.at[pl.ds(0, 2)], in_sem.at[1]),
        pltpu.make_async_copy(transfer.at[pl.ds(half + dom, 1)], par.at[pl.ds(2, 1)], in_sem.at[2]),
        pltpu.make_async_copy(transfer.at[pl.ds(half + doms + dom // 2, 1)], par.at[pl.ds(3, 1)], in_sem.at[3]),
        pltpu.make_async_copy(transfer.at[pl.ds(nodes - 2, 1)], par.at[pl.ds(4, 1)], in_sem.at[4]),
    ]
    for level in range(top_levels):
        step = 2 << level
        middle = leaf // step * step + step // 2
        loads.append(pltpu.make_async_copy(toptr.at[pl.ds(middle, 1)], par.at[pl.ds(5 + level, 1)], in_sem.at[5 + level]))
    for load in loads:
        load.start()

    def near(step):
        return lax.rem(leaf + step + leaves, leaves)

    steps = [s for s in range(-REACH, REACH + 1) if s]
    barrier = pltpu.get_barrier_semaphore()
    for k in range(1, doms):
        pl.semaphore_signal(barrier, inc=1, device_id=(leaf, lax.rem(dom + k, doms)), device_id_type=MESH)
    for s in steps:
        pl.semaphore_signal(barrier, inc=1, device_id=(near(s), dom), device_id_type=MESH)
    for level in range(top_levels):
        other = leaf + (1 - 2 * lax.rem(leaf // (1 << level), 2)) * (1 << level)
        pl.semaphore_signal(barrier, inc=1, device_id=(other, dom), device_id_type=MESH)

    lane = lax.broadcasted_iota(jnp.int32, (K, 128), 1)
    left = lane < K
    side = lane // K

    stacked = [child[n] for n in range(per)]
    current = factor([dot(x, x, NT) for x in stacked])
    for m in range(per // 2):
        tall = jnp.concatenate([current[2 * m][:, :K], current[2 * m + 1][:, :K]], axis=0)
        win[REACH, per // 2 * dom + m] = tall.T
    pl.semaphore_wait(barrier, doms - 1 + len(steps) + top_levels)
    mine = win.at[REACH, pl.ds(per // 2 * dom, per // 2)]
    gather = []
    for k in range(1, doms):
        copy = pltpu.make_async_remote_copy(
            src_ref=mine, dst_ref=mine, send_sem=gs.at[k - 1], recv_sem=gr.at[k - 1],
            device_id=(leaf, lax.rem(dom + k, doms)), device_id_type=MESH)
        copy.start()
        gather.append(copy)
    for n in range(per):
        bottom_out[n] = dot(pltpu.roll(current[n], K, 1)[:, :K], stacked[n], NN)

    for load in loads:
        load.wait()
    for n in range(5 + top_levels):
        pair = par[n]
        par[n] = jnp.concatenate([pair[:, :K], pltpu.roll(pair, K, 1)[:, :K]], axis=0).T

    def product(packed, n):
        wide = jnp.concatenate([jnp.where(left, packed, 0.0), jnp.where(left, 0.0, packed)], axis=0)
        return dot(par[n], wide, NT)

    xa = [product(jnp.where(left, current[2 * s], pltpu.roll(current[2 * s + 1], K, 1)), s) for s in range(per // 2)]
    current = factor([dot(x, x, NT) for x in xa])
    for s in range(per // 2):
        local_out[per // 2 * dom + s] = dot(pltpu.roll(current[s], K, 1)[:, :K], xa[s], NN)
    spread = []
    for k in range(1, doms):
        view = local_out.at[pl.ds(per // 2 * dom, per // 2)]
        copy = pltpu.make_async_remote_copy(
            src_ref=view, dst_ref=view, send_sem=bs.at[k - 1], recv_sem=br.at[k - 1],
            device_id=(leaf, lax.rem(dom + k, doms)), device_id_type=MESH)
        copy.start()
        spread.append(copy)
    x = product(jnp.where(left, current[0], pltpu.roll(current[1], K, 1)), 2)
    (factored,) = factor([dot(x, x, NT)])
    local_out[half + dom] = dot(pltpu.roll(factored, K, 1)[:, :K], x, NN)
    for k in range(1, doms):
        view = local_out.at[pl.ds(half + dom, 1)]
        copy = pltpu.make_async_remote_copy(
            src_ref=view, dst_ref=view, send_sem=cs.at[k - 1], recv_sem=cr.at[k - 1],
            device_id=(leaf, lax.rem(dom + k, doms)), device_id_type=MESH)
        copy.start()
        spread.append(copy)

    for copy in gather:
        copy.wait_recv()
    window = []
    for j, s in enumerate(steps):
        copy = pltpu.make_async_remote_copy(
            src_ref=win.at[REACH], dst_ref=win.at[REACH - s], send_sem=ws.at[j], recv_sem=wr.at[j],
            device_id=(near(s), dom), device_id_type=MESH)
        copy.start()
        window.append(copy)

    def exchange(e, other, bit, factored, hook=None):
        rolled = pltpu.roll(factored, K, 1)
        shaped = jnp.where(bit == 0, factored, rolled)
        xs[e] = shaped
        copy = pltpu.make_async_remote_copy(
            src_ref=xs.at[e], dst_ref=xr.at[e], send_sem=es.at[e], recv_sem=er.at[e],
            device_id=other, device_id_type=MESH)
        copy.start()
        copy.wait_recv()
        x = product(jnp.where(side == bit, shaped, xr[e]), 3 + e)
        (factored,) = factor([dot(x, x, NT)], hook)
        return factored, dot(pltpu.roll(factored, K, 1)[:, :K], x, NN)

    bit = lax.rem(dom, 2)
    factored, basis = exchange(0, (leaf, dom + 1 - 2 * bit), bit, factored)
    place = half + doms + dom // 2
    local_out[place] = basis
    view = local_out.at[pl.ds(place, 1)]
    copy = pltpu.make_async_remote_copy(
        src_ref=view, dst_ref=view, send_sem=ds, recv_sem=dr,
        device_id=(leaf, lax.rem(dom + 2, doms)), device_id_type=MESH)
    copy.start()
    spread.append(copy)
    bit = dom // 2
    factored, basis = exchange(1, (leaf, dom + (1 - 2 * bit) * 2), bit, factored)
    local_out[nodes - 2] = basis

    top_out[0] = jnp.zeros((K, 128), F32)

    def climb(level, factored):
        step = jnp.int32(1)
        for r in range(1, top_levels):
            step = jnp.where(level == r, 1 << r, step)
        bit = lax.rem(leaf // step, 2)
        factored, basis = exchange(dom_levels + level, (leaf + (1 - 2 * bit) * step, dom), bit, factored)
        middle = leaf // (2 * step) * (2 * step) + step
        top_out[0] = jnp.where(middle == leaf, basis, top_out[0])
        return factored

    factored = lax.fori_loop(0, top_levels, climb, factored)
    root_out[...] = factored[:, :K]

    coup_copy.wait()

    def turn(i, carry):
        slab = jnp.concatenate([ct[i, :, 0:128], ct[i, :, 128:256]], axis=0)
        turned[pl.ds(i, 128, K), :] = slab.T
        return carry

    lax.fori_loop(0, K, turn, 0, unroll=4)

    def expand_rows(m, carry):
        pair = win[REACH, m]
        both = jnp.concatenate([pair, pair], axis=0).T
        high = both.astype(BF)
        low = jnp.where(lax.broadcasted_iota(jnp.int32, (128, 128), 1) < K, both - high.astype(F32), 0.0).astype(BF)
        for h in range(2):
            us[2 * m + h, :, 0:128] = high[K * h : K * h + K]
            us[2 * m + h, :, 128:256] = low[K * h : K * h + K]
        return carry

    lax.fori_loop(0, half, expand_rows, 0, unroll=2)

    def row_side(b, carry):
        off = pl.multiple_of(b * K, K)
        high, low = split(turned[pl.ds(off, K), :])
        weights = jnp.concatenate([high, low, high, jnp.zeros_like(high)], axis=0)
        first = lax.rem(rows[b], nodes)
        second = lax.rem(rows[b + 128], nodes)
        both = dot16(jnp.concatenate([us[first], us[second]], axis=0), weights)
        turned[pl.ds(off, K), :] = jnp.where(left, both[:K], both[K:])
        return carry

    lax.fori_loop(0, 128, row_side, 0, unroll=8)

    for copy in window:
        copy.wait_recv()

    def expand_cols(q, carry):
        s = q // half
        m = q % half
        pair = win[s, m]
        rolled = pltpu.roll(pair, K, 1)
        for h, (a, b) in enumerate(((pair, rolled), (rolled, pair))):
            for ref, value in ((lw, jnp.where(left, a, 0.0)), (rw, jnp.where(left, 0.0, b))):
                high, low = split(value)
                ref[2 * q + h, :, 0:128] = high
                ref[2 * q + h, :, 128:256] = low
        return carry

    lax.fori_loop(0, (2 * REACH + 1) * half, expand_cols, 0, unroll=4)

    def col_side(b, carry):
        off = pl.multiple_of(b * K, K)
        high, low = split(turned[pl.ds(off, K), :])
        first = jnp.clip(cols[b] - (leaf - REACH) * nodes, 0, last)
        second = jnp.clip(cols[b + 128] - (leaf - REACH) * nodes, 0, last)
        weights = jnp.concatenate([lw[first], rw[second]], axis=0)
        both = dot16(jnp.concatenate([high, low], axis=0), weights)
        turned[pl.ds(off, K), :] = both[:K, :128] + both[K:, :128] + both[:K, 128:]
        return carry

    lax.fori_loop(0, 128, col_side, 0, unroll=8)

    def turn_back(i, carry):
        slab = turned[pl.ds(i, 128, K), :].T
        ct[i, :, 0:128] = slab[:K]
        ct[i, :, 128:256] = slab[K:]
        return carry

    parts = 4
    stores = []
    for part in range(parts):
        lax.fori_loop(K // parts * part, K // parts * (part + 1), turn_back, 0, unroll=4)
        span = pl.ds(K // parts * part, K // parts)
        copy = pltpu.make_async_copy(ct.at[span], proj_out.at[span], out_sem.at[part])
        copy.start()
        stores.append(copy)
    for copy in stores:
        copy.wait()

    for copy in spread:
        copy.wait_recv()
    for copy in gather + spread + window:
        copy.wait_send()

    def drain(e, carry):
        pltpu.make_async_remote_copy(
            src_ref=xs.at[e], dst_ref=xr.at[e], send_sem=es.at[e], recv_sem=er.at[e],
            device_id=(leaf, dom), device_id_type=MESH).wait_send()
        return carry

    lax.fori_loop(0, dom_levels + top_levels, drain, 0)


def on_device(doms, leaves, child_terms, transfer, top_transfer, coupling, block_row, block_col):
    per = child_terms.shape[0]
    nodes = per * doms
    top_levels = leaves.bit_length() - 1
    exchanges = top_levels + doms.bit_length() - 1
    vmem = pl.BlockSpec(memory_space=pltpu.VMEM)
    smem = pl.BlockSpec(memory_space=pltpu.SMEM)
    hbm = pl.BlockSpec(memory_space=pl.ANY)
    dma = pltpu.SemaphoreType.DMA
    sides = 2 * REACH
    bottom, local, top, root, projected = pl.pallas_call(
        functools.partial(kernel, doms, leaves),
        out_shape=(
            jax.ShapeDtypeStruct((per, K, 2 * K), F32),
            jax.ShapeDtypeStruct((nodes - 1, K, 2 * K), F32),
            jax.ShapeDtypeStruct((1, K, 2 * K), F32),
            jax.ShapeDtypeStruct((K, K), F32),
            jax.ShapeDtypeStruct((K, K, 256), F32),
        ),
        in_specs=[vmem, hbm, hbm, hbm, smem, smem],
        out_specs=(vmem, vmem, vmem, vmem, hbm),
        scratch_shapes=[
            pltpu.VMEM((sides + 1, nodes // 2, K, 128), F32),
            pltpu.VMEM((K, K, 256), F32),
            pltpu.VMEM((5 + top_levels, K, 128), F32),
            pltpu.VMEM((128 * K, 128), F32),
            pltpu.VMEM((nodes, K, 256), BF),
            pltpu.VMEM(((sides + 1) * nodes, K, 256), BF),
            pltpu.VMEM(((sides + 1) * nodes, K, 256), BF),
            pltpu.VMEM((exchanges, K, 128), F32),
            pltpu.VMEM((exchanges, K, 128), F32),
            dma((5 + top_levels,)),
            dma((4,)),
            dma((doms - 1,)), dma((doms - 1,)),
            dma((sides,)), dma((sides,)),
            dma((doms - 1,)), dma((doms - 1,)),
            dma((doms - 1,)), dma((doms - 1,)),
            dma, dma,
            dma((exchanges,)), dma((exchanges,)),
        ],
        compiler_params=pltpu.CompilerParams(
            collective_id=0, has_side_effects=True, vmem_limit_bytes=48 * 2**20),
    )(child_terms, transfer, top_transfer, jnp.transpose(coupling, (1, 2, 0)), block_row, block_col)
    return bottom, local, top, root, jnp.transpose(projected, (2, 0, 1))


def solution(mesh):
    split_all = P(("leaf", "dom"), None, None)
    placed = (split_all, P("leaf", None, None), P(), split_all, P(("leaf", "dom")), P(("leaf", "dom")))
    return jax.shard_map(
        functools.partial(on_device, mesh.shape["dom"], mesh.shape["leaf"]),
        mesh=mesh,
        in_specs=placed,
        out_specs=(split_all, P("leaf", None, None), P("leaf", None, None), P(), split_all),
        check_vma=False,
    )
```

profile of v0, /device:TPU:1, one launch (start us, length us, event | category | flops | bytes accessed | tf_op | source)
XLA Modules:
  0.0 98.6 jit_solution(18313300310120174063)
XLA Ops:
  0.6 0.0 copy-start
  0.6 1.6 %copy-done = f32[64,64,128]{2,1,0:T(8,128)S(1)} copy-done((f32[64,64,128]{2,1,0:T(8,128)S(1)}, f32[64,64,128]{2,1,0:T(8,128)}, u32[]{:S(2)}) %copy-start) | copy-done | bytes 2097176
  2.2 0.0 copy-start.1
  2.2 1.0 %copy-done.1 = f32[15,64,128]{2,1,0:T(8,128)S(1)} copy-done((f32[15,64,128]{2,1,0:T(8,128)S(1)}, f32[15,64,128]{2,1,0:T(8,128)}, u32[]{:S(2)}) %copy-start.1) | copy-done | bytes 491544
  3.3 0.0 copy-start.2
  3.3 0.9 copy-done.2
  4.2 0.0 copy-start.3
  4.2 0.7 copy-done.3
  4.8 0.0 copy-start.4
  4.8 0.7 copy-done.4
  5.5 85.7 %shard_map.101 = (f32[4,64,128]{2,1,0:T(8,128)S(1)}, f32[15,64,128]{2,1,0:T(8,128)S(1)}, f32[1,64,128]{2,1,0:T(8,128)S(1)}, f32[64,64]{1,0:T(8,128)S(1)}, f32[64,64,256]{2,1,0:T(8,128)}) custom-call(f32[4,64,128]{2,1,0:T(8,128)S(1)} %copy-done.2, f32[15,64,128]{2,1,0:T(8,128)S(1)} %copy-done.1, f32[64,64,128]{2,1,0:T(8,128)S(1)} %copy-done, ...), custom_call_target="tpu_custom_call" | custom-call | tf_op jit(solution)/shard_map/pallas_call | solution.py:317
  91.3 0.7 copy.16
  91.9 0.8 copy.17
  92.7 0.6 copy.18
  93.3 0.6 copy.19
  93.9 4.7 %copy.20 = f32[256,64,64]{0,2,1:T(8,128)} copy(f32[256,64,64]{0,2,1:T(8,128)} %bitcast.3) | data formatting | bytes 8388608
Async XLA Ops:
  0.6 1.6 %copy-start = (f32[64,64,128]{2,1,0:T(8,128)S(1)}, f32[64,64,128]{2,1,0:T(8,128)}, u32[]{:S(2)}) copy-start(f32[64,64,128]{2,1,0:T(8,128)} %toptr.1) | copy-start | bytes 6291460
  2.2 1.0 %copy-start.1 = (f32[15,64,128]{2,1,0:T(8,128)S(1)}, f32[15,64,128]{2,1,0:T(8,128)}, u32[]{:S(2)}) copy-start(f32[15,64,128]{2,1,0:T(8,128)} %transfer.1) | copy-start | bytes 1474564
  3.3 0.9 copy-start.2
  4.2 0.7 copy-start.3
  4.8 0.7 copy-start.4
where the time goes:
time: 100 us; the launch traced here: 98.6 us
  Pallas kernels  85.7 us (86%)
  local copies, waits for them, and re-layouts  12.2 us (12%)
    pallas_call x1, Pallas kernels, on_device(): pl.pallas_call(functools.partial(kernel, doms, leaves), out_shape=(jax.Sh...  85.7 us
    unnamed x15, local copies, waits for them, and re-layouts  12.2 us

commit v1 on v0

v1 whole, which is shorter than its diff:
```python
import functools
import itertools

import jax
import jax.numpy as jnp
from jax import lax
from jax.experimental import pallas as pl
from jax.experimental.pallas import tpu as pltpu
from jax.sharding import PartitionSpec as P

REACH = 3
K = 64
F32 = jnp.float32
BF = jnp.bfloat16
HIGH = lax.Precision.HIGHEST
MESH = pl.DeviceIdType.MESH
NN = ((1,), (0,))
NT = ((1,), (1,))


def dot(a, b, dims):
    return lax.dot_general(a, b, (dims, ((), ())), precision=HIGH, preferred_element_type=F32)


def dot16(a, b):
    return lax.dot_general(a, b, (NN, ((), ())), preferred_element_type=F32)


def split(x):
    high = x.astype(BF)
    return high, (x - high.astype(F32)).astype(BF)


def factor(grams, hook=None):
    count = len(grams)
    sub = lax.broadcasted_iota(jnp.int32, (1, 8, 128), 1)
    row = lax.broadcasted_iota(jnp.int32, (K, K), 0)
    col = lax.broadcasted_iota(jnp.int32, (K, K), 1)
    eye = jnp.where(row == col, 1.0, 0.0).astype(F32)
    rest = jnp.stack([jnp.concatenate([g, eye], axis=1) for g in grams])
    done = []
    for p in range(8):
        panel = rest[:, :8]
        rest = rest[:, 8:]
        left = 56 - 8 * p
        lanes = [8 * p + c for c in range(8)]
        cols = [jnp.broadcast_to(panel[:, :, c : c + 1], (count, 8, 128)) for c in lanes]
        below = [jnp.broadcast_to(rest[:, :, c : c + 1], (count, left, 128)) for c in lanes] if left else []
        out = jnp.zeros((count, 8, 128), F32)
        for k in range(8):
            here = sub == k
            pivot_row = jnp.broadcast_to(panel[:, k : k + 1, :], (count, 8, 128))
            heads = [jnp.broadcast_to(c[:, k : k + 1, :], (count, 8, 128)) for c in cols[k:]]
            out = jnp.where(here, pivot_row * lax.rsqrt(heads[0]), out)
            scale = jnp.where(here, -1.0, cols[k]) * (1.0 / heads[0])
            panel = jnp.where(here, 0.0, panel) - scale * pivot_row
            for c in range(k + 1, 8):
                cols[c] = jnp.where(here, 0.0, cols[c]) - scale * heads[c - k]
        done.append(out)
        for k in range(8 if left else 0):
            rest = rest - below[k] * jnp.broadcast_to(panel[:, k : k + 1, :], (count, left, 128))
        if hook is not None:
            hook(p)
    keep = lax.broadcasted_iota(jnp.int32, (K, 128), 1) >= lax.broadcasted_iota(jnp.int32, (K, 128), 0)
    return [jnp.where(keep, jnp.concatenate([d[n] for d in done], axis=0), 0.0) for n in range(count)]


def kernel(doms, leaves, child_hbm, transfer, toptr, coup, rows_hbm, cols_hbm,
           bottom_hbm, local_hbm, top_hbm, root_hbm, turned_hbm,
           bottom_out, local_out, top_out, root_out, turned,
           child, rows, cols, win, ct, par, us, lw, rw, xr,
           in_sem, out_sem, gs, gr, ws, wr, bs, br, cs, cr, es, er):
    leaf = lax.axis_index("leaf")
    dom = lax.axis_index("dom")
    top_levels = leaves.bit_length() - 1
    dom_levels = doms.bit_length() - 1
    stages = (top_levels + dom_levels) // 2
    per = child.shape[0]
    nodes = per * doms
    half = nodes // 2
    own = per // 2
    last = (2 * REACH + 1) * nodes - 1

    child_copy = pltpu.make_async_copy(child_hbm, child, in_sem.at[0])
    child_copy.start()
    loads = [
        pltpu.make_async_copy(transfer.at[pl.ds(own * dom, own)], par.at[pl.ds(0, own)], in_sem.at[1]),
        pltpu.make_async_copy(transfer.at[pl.ds(half + dom, 1)], par.at[pl.ds(2, 1)], in_sem.at[2]),
        pltpu.make_async_copy(transfer.at[pl.ds(half + doms, 3)], par.at[pl.ds(3, 3)], in_sem.at[3]),
    ]
    bases = []
    for t in range(stages - 1):
        step = 4**t
        base = leaf // (4 * step) * (4 * step)
        bases.append([base + step * r for r in (1, 3, 2)])
        for r in range(3):
            n = 3 * (t + 2) + r
            loads.append(pltpu.make_async_copy(toptr.at[pl.ds(bases[t][r], 1)], par.at[pl.ds(n, 1)], in_sem.at[n - 2]))
    for load in loads:
        load.start()
    index_loads = [
        pltpu.make_async_copy(rows_hbm, rows, in_sem.at[3 * stages + 1]),
        pltpu.make_async_copy(cols_hbm, cols, in_sem.at[3 * stages + 2]),
    ]
    for load in index_loads:
        load.start()
    coup_copy = pltpu.make_async_copy(coup, ct, in_sem.at[3 * stages + 3])
    coup_copy.start()

    def near(step):
        return lax.rem(leaf + step + leaves, leaves)

    def dom_peer(step):
        return (leaf, lax.rem(dom + step, doms))

    steps = [s for s in range(-REACH, REACH + 1) if s]
    groups = [(dom, [dom_peer(k) for k in range(1, 4)])]
    for t in range(stages - 1):
        step = 4**t
        spot = lax.rem(leaf // step, 4)
        groups.append((spot, [(leaf + (lax.rem(spot + k, 4) - spot) * step, dom) for k in range(1, 4)]))
    greeted = [(near(s), dom) for s in steps]
    for _, others in groups:
        greeted += others
    barrier = pltpu.get_barrier_semaphore()
    for other in greeted:
        pl.semaphore_signal(barrier, inc=1, device_id=other, device_id_type=MESH)

    lane = lax.broadcasted_iota(jnp.int32, (K, 128), 1)
    left = lane < K
    started = []

    def send(src, dst, send_sem, recv_sem, other):
        copy = pltpu.make_async_remote_copy(
            src_ref=src, dst_ref=dst, send_sem=send_sem, recv_sem=recv_sem,
            device_id=other, device_id_type=MESH)
        copy.start()
        started.append(copy)
        return copy

    def spread(view, send_sems, recv_sems):
        return [send(view, view, send_sems.at[k - 1], recv_sems.at[k - 1], dom_peer(k)) for k in range(1, doms)]

    def inverse(factored):
        return pltpu.roll(factored, K, 1)[:, :K]

    def turn(i, carry):
        slab = jnp.concatenate([ct[i, :, 0:128], ct[i, :, 128:256]], axis=0)
        turned[pl.ds(i, 128, K), :] = slab.T
        return carry

    def expand_rows(m, carry):
        pair = win[REACH, m]
        both = jnp.concatenate([pair, pair], axis=0).T
        high = both.astype(BF)
        low = jnp.where(lax.broadcasted_iota(jnp.int32, (128, 128), 1) < K, both - high.astype(F32), 0.0).astype(BF)
        for h in range(2):
            us[2 * m + h, :, 0:128] = high[K * h : K * h + K]
            us[2 * m + h, :, 128:256] = low[K * h : K * h + K]
        return carry

    def row_side(b, carry):
        off = pl.multiple_of(b * K, K)
        high, low = split(turned[pl.ds(off, K), :])
        weights = jnp.concatenate([high, low, high, jnp.zeros_like(high)], axis=0)
        first = lax.rem(rows[b], nodes)
        second = lax.rem(rows[b + 128], nodes)
        both = dot16(jnp.concatenate([us[first], us[second]], axis=0), weights)
        turned[pl.ds(off, K), :] = jnp.where(left, both[:K], both[K:])
        return carry

    def expand_cols(q, carry):
        s = q // half
        m = q % half
        pair = win[s, m]
        rolled = pltpu.roll(pair, K, 1)
        for h, (a, b) in enumerate(((pair, rolled), (rolled, pair))):
            for ref, value in ((lw, jnp.where(left, a, 0.0)), (rw, jnp.where(left, 0.0, b))):
                high, low = split(value)
                ref[2 * q + h, :, 0:128] = high
                ref[2 * q + h, :, 128:256] = low
        return carry

    def col_side(b, carry):
        off = pl.multiple_of(b * K, K)
        high, low = split(turned[pl.ds(off, K), :])
        first = jnp.clip(cols[b] - (leaf - REACH) * nodes, 0, last)
        second = jnp.clip(cols[b + 128] - (leaf - REACH) * nodes, 0, last)
        weights = jnp.concatenate([lw[first], rw[second]], axis=0)
        both = dot16(jnp.concatenate([high, low], axis=0), weights)
        turned[pl.ds(off, K), :] = both[:K, :128] + both[K:, :128] + both[:K, 128:]
        return carry

    def run(body, first, past, unroll):
        lax.fori_loop(first, past, body, 0, unroll=unroll)

    pairs = (2 * REACH + 1) * half
    window = []

    def prepare():
        for load in index_loads:
            load.wait()
        for arrival in gather:
            arrival.wait_recv()
        for j, s in enumerate(steps):
            window.append(send(win.at[REACH], win.at[REACH - s], ws.at[j], wr.at[j], (near(s), dom)))
        run(expand_rows, 0, half, 2)

    def widen():
        for copy in window:
            copy.wait_recv()
        run(expand_cols, 0, pairs, 4)

    queues = {"turn": iter(range(K)), "row": iter(range(128)), "col": iter(range(128))}
    bodies = {"turn": turn, "row": row_side, "col": col_side}

    def hook(kind, count):
        def emit(_):
            for _ in range(count):
                n = next(queues[kind], None)
                if n is not None:
                    bodies[kind](n, 0)
        return emit

    def chunk(kind, count, unroll):
        taken = list(itertools.islice(queues[kind], count))
        run(bodies[kind], taken[0], taken[-1] + 1, unroll)

    def fill(stage):
        if stage == 0:
            chunk("turn", 32, 4)
            prepare()
        elif stage == stages - 3:
            chunk("row", 48, 8)
        elif stage == stages - 2:
            chunk("row", None, 8)
            widen()
        elif stage == stages - 1:
            chunk("col", 48, 8)

    hooks = {0: ("row", 2, 2), stages - 3: ("row", 2, 2), stages - 2: ("col", 2, 2), stages - 1: ("col", 6, 0)}

    child_copy.wait()
    stacked = [child[n] for n in range(per)]
    current = factor([dot(x, x, NT) for x in stacked])
    for m in range(own):
        tall = jnp.concatenate([current[2 * m][:, :K], current[2 * m + 1][:, :K]], axis=0)
        win[REACH, own * dom + m] = tall.T
    pl.semaphore_wait(barrier, len(greeted))
    mine = win.at[REACH, pl.ds(own * dom, own)]
    gather = spread(mine, gs, gr)

    for load in loads:
        load.wait()
    for n in range(3 * stages + 3):
        pair = par[n]
        par[n] = jnp.concatenate([pair[:, :K], pltpu.roll(pair, K, 1)[:, :K]], axis=0).T

    def product(packed, n):
        wide = jnp.concatenate([jnp.where(left, packed, 0.0), jnp.where(left, 0.0, packed)], axis=0)
        return dot(par[n], wide, NT)

    xa = [product(jnp.where(left, current[2 * s], pltpu.roll(current[2 * s + 1], K, 1)), s) for s in range(own)]
    below = current
    coup_copy.wait()
    current = factor([dot(x, x, NT) for x in xa], hook("turn", 2))
    x = product(jnp.where(left, current[0], pltpu.roll(current[1], K, 1)), own)
    for n in range(per):
        bottom_out[n] = dot(inverse(below[n]), stacked[n], NN)
    stores = [pltpu.make_async_copy(bottom_out, bottom_hbm, out_sem.at[0])]
    stores[0].start()
    for s in range(own):
        local_out[own * dom + s] = dot(inverse(current[s]), xa[s], NN)
    arrivals = spread(local_out.at[pl.ds(own * dom, own)], bs, br)
    (factored,) = factor([dot(x, x, NT)], hook("turn", 2))

    top_out[0] = jnp.zeros((K, 128), F32)

    def keep_bases(stage, lowers, xs, top, x):
        if stage == 0:
            for r, (lower, value) in enumerate(zip(lowers + [top], xs + [x])):
                local_out[half + doms + r] = dot(inverse(lower), value, NN)
            return
        first, second, middle = bases[stage - 1]
        at_first, at_middle = first == leaf, middle == leaf
        lower = jnp.where(at_middle, top, jnp.where(at_first, lowers[0], lowers[1]))
        value = jnp.where(at_middle, x, jnp.where(at_first, xs[0], xs[1]))
        found = at_first | at_middle | (second == leaf)
        top_out[0] = jnp.where(found, dot(inverse(lower), value, NN), top_out[0])

    pending = None
    for stage in range(stages):
        spot, others = groups[stage]
        xr[stage, spot] = jnp.where(lax.rem(spot, 2) == 0, factored, pltpu.roll(factored, K, 1))
        view = xr.at[stage, spot]
        copies = [send(view, view, es.at[stage, k], er.at[stage, k], others[k]) for k in range(3)]
        if stage == 0:
            local_out[half + dom] = dot(inverse(factored), x, NN)
            arrivals += spread(local_out.at[pl.ds(half + dom, 1)], cs, cr)
        else:
            keep_bases(*pending)
        fill(stage)
        for copy in copies:
            copy.wait_recv()
        kind, low, high = hooks.get(stage, ("row", 0, 0))
        xs = [product(jnp.where(left, xr[stage, 2 * s], xr[stage, 2 * s + 1]), 3 * stage + 3 + s) for s in range(2)]
        lowers = factor([dot(v, v, NT) for v in xs], hook(kind, low))
        if stage == stages - 1:
            stores.append(pltpu.make_async_copy(turned, turned_hbm, out_sem.at[1]))
            stores[-1].start()
            for copy in arrivals:
                copy.wait_recv()
            stores.append(pltpu.make_async_copy(local_out, local_hbm, out_sem.at[2]))
            stores[-1].start()
        x = product(jnp.where(left, lowers[0], pltpu.roll(lowers[1], K, 1)), 3 * stage + 5)
        (factored,) = factor([dot(x, x, NT)], hook(kind, high))
        pending = (stage, lowers, xs, factored, x)
    root_out[...] = factored[:, :K]
    stores.append(pltpu.make_async_copy(root_out, root_hbm, out_sem.at[3]))
    stores[-1].start()
    keep_bases(*pending)
    stores.append(pltpu.make_async_copy(top_out, top_hbm, out_sem.at[4]))
    stores[-1].start()

    for copy in started:
        copy.wait_send()
    for copy in stores:
        copy.wait()


def finish(bottom, local, top, root, turned, bottom_out, local_out, top_out, root_out, proj_out,
           bottom_in, local_in, top_in, root_in, parts_in, ct, load_sem, part_sem, store_sem, out_sem):
    parts, _, deep, _ = parts_in.shape
    part_loads = []
    for part in range(parts):
        copy = pltpu.make_async_copy(turned.at[:, pl.ds(deep * part, deep)], parts_in.at[part], part_sem.at[part])
        copy.start()
        part_loads.append(copy)
    small = ((bottom, bottom_in, bottom_out), (local, local_in, local_out), (top, top_in, top_out), (root, root_in, root_out))
    loads = [pltpu.make_async_copy(src, mid, load_sem.at[n]) for n, (src, mid, _) in enumerate(small)]
    stores = [pltpu.make_async_copy(mid, dst, store_sem.at[n]) for n, (_, mid, dst) in enumerate(small)]
    for load in loads:
        load.start()
    for part in range(parts):
        part_loads[part].wait()
        for r in range(deep):
            slab = parts_in[part, :, r, :].T
            ct[deep * part + r, :, 0:128] = slab[:K]
            ct[deep * part + r, :, 128:256] = slab[K:]
        span = pl.ds(deep * part, deep)
        copy = pltpu.make_async_copy(ct.at[span], proj_out.at[span], out_sem.at[part])
        copy.start()
        stores.append(copy)
        if part == 0:
            for load, store in zip(loads, stores):
                load.wait()
                store.start()
    for copy in stores:
        copy.wait()


def on_device(doms, leaves, child_terms, transfer, top_transfer, coupling, block_row, block_col):
    per = child_terms.shape[0]
    nodes = per * doms
    top_levels = leaves.bit_length() - 1
    stages = (top_levels + doms.bit_length() - 1) // 2
    hbm = pl.BlockSpec(memory_space=pltpu.HBM)
    dma = pltpu.SemaphoreType.DMA
    sides = 2 * REACH
    small_shapes = ((per, K, 2 * K), (nodes - 1, K, 2 * K), (1, K, 2 * K), (K, K))
    small = tuple(jax.ShapeDtypeStruct(shape, F32) for shape in small_shapes)
    small_scratch = [pltpu.VMEM(shape, F32) for shape in small_shapes]
    *ready, turned = pl.pallas_call(
        functools.partial(kernel, doms, leaves),
        out_shape=small + (jax.ShapeDtypeStruct((128 * K, 128), F32),),
        in_specs=[hbm] * 6,
        out_specs=(hbm,) * 5,
        scratch_shapes=small_scratch + [
            pltpu.VMEM((128 * K, 128), F32),
            pltpu.VMEM((per, K, 128), F32),
            pltpu.SMEM((256,), jnp.int32),
            pltpu.SMEM((256,), jnp.int32),
            pltpu.VMEM((sides + 1, nodes // 2, K, 128), F32),
            pltpu.VMEM((K, K, 256), F32),
            pltpu.VMEM((3 * stages + 3, K, 128), F32),
            pltpu.VMEM((nodes, K, 256), BF),
            pltpu.VMEM(((sides + 1) * nodes, K, 256), BF),
            pltpu.VMEM(((sides + 1) * nodes, K, 256), BF),
            pltpu.VMEM((stages, 4, K, 128), F32),
            dma((3 * stages + 4,)),
            dma((5,)),
            dma((doms - 1,)), dma((doms - 1,)),
            dma((sides,)), dma((sides,)),
            dma((doms - 1,)), dma((doms - 1,)),
            dma((doms - 1,)), dma((doms - 1,)),
            dma((stages, 3)), dma((stages, 3)),
        ],
        compiler_params=pltpu.CompilerParams(
            collective_id=0, has_side_effects=True, vmem_limit_bytes=60 * 2**20),
    )(child_terms, transfer, top_transfer, jnp.transpose(coupling, (1, 2, 0)), block_row, block_col)
    bottom, local, top, root, projected = pl.pallas_call(
        finish,
        out_shape=small + (jax.ShapeDtypeStruct((K, K, 256), F32),),
        in_specs=[hbm] * 5,
        out_specs=(hbm,) * 5,
        scratch_shapes=small_scratch + [
            pltpu.VMEM((4, 128, K // 4, 128), F32), pltpu.VMEM((K, K, 256), F32),
            dma((4,)), dma((4,)), dma((4,)), dma((4,)),
        ],
        compiler_params=pltpu.CompilerParams(vmem_limit_bytes=60 * 2**20),
    )(*ready, turned.reshape(128, K, 128))
    return bottom, local, top, root, jnp.transpose(projected, (2, 0, 1))


def solution(mesh):
    split_all = P(("leaf", "dom"), None, None)
    placed = (split_all, P("leaf", None, None), P(), split_all, P(("leaf", "dom")), P(("leaf", "dom")))
    return jax.shard_map(
        functools.partial(on_device, mesh.shape["dom"], mesh.shape["leaf"]),
        mesh=mesh,
        in_specs=placed,
        out_specs=(split_all, P("leaf", None, None), P("leaf", None, None), P(), split_all),
        check_vma=False,
    )
```

time: 100 us -> 74.6 us (0.75)
  the two profiles are of different devices: /device:TPU:1 before, /device:TPU:2 now
where the time goes in v1:
time: 74.6 us; the launch traced here: 74.5 us
  Pallas kernels  73.7 us (99%)
  between operations  0.82 us (1%)
    pallas_call x1, Pallas kernels, on_device(): pl.pallas_call(functools.partial(kernel, doms, leaves), out_shape=small +...  68.5 us
    pallas_call x1, Pallas kernels, on_device(): pl.pallas_call(finish, out_shape=small + (jax.ShapeDtypeStruct((K, K, 256...  5.24 us

profile of v1, /device:TPU:2, one launch (start us, length us, event | category | flops | bytes accessed | tf_op | source)
XLA Modules:
  0.0 74.5 jit_solution(17324420162415716670)
XLA Ops:
  0.6 68.5 %shard_map.101 = (f32[4,64,128]{2,1,0:T(8,128)}, f32[15,64,128]{2,1,0:T(8,128)}, f32[1,64,128]{2,1,0:T(8,128)}, f32[64,64]{1,0:T(8,128)}, f32[8192,128]{1,0:T(8,128)}) custom-call(f32[4,64,128]{2,1,0:T(8,128)} %child_hbm.1, f32[15,64,128]{2,1,0:T(8,128)} %transfer.1, f32[64,64,128]{2,1,0:T(8,128)} %toptr.1, f32[64,64,256]{2,1,0:T(8,128)} %bitcast.3, ...), custom_call_target="tpu_custom_call" | custom-call | tf_op jit(solution)/shard_map/pallas_call | solution.py:373
  69.1 5.2 %shard_map.102 = (f32[4,64,128]{2,1,0:T(8,128)}, f32[15,64,128]{2,1,0:T(8,128)}, f32[1,64,128]{2,1,0:T(8,128)}, f32[64,64]{1,0:T(8,128)}, f32[64,64,256]{2,1,0:T(8,128)}) custom-call(f32[4,64,128]{2,1,0:T(8,128)} %get-tuple-element.15.bottom, f32[15,64,128]{2,1,0:T(8,128)} %get-tuple-element.16.local, f32[1,64,128]{2,1,0:T(8,128)} %get-tuple-element.17.top, ...), custom_call_target="tpu_custom_call" | custom-call | tf_op jit(solution)/shard_map/pallas_call | solution.py:401

commit v2 on v1

--- a/solution.py
+++ b/solution.py
@@ -31,38 +31,70 @@
     return high, (x - high.astype(F32)).astype(BF)
 
 
+WIDE = 16
+TURN_FILL = 32
+ROW_FILL = 48
+ROW_HOOK = 16
+COL_FILL = 48
+COL_HOOK = 48
+
+
 def factor(grams, hook=None):
-    count = len(grams)
-    sub = lax.broadcasted_iota(jnp.int32, (1, 8, 128), 1)
+    full = (WIDE, 128)
+    sub = lax.broadcasted_iota(jnp.int32, full, 0)
     row = lax.broadcasted_iota(jnp.int32, (K, K), 0)
     col = lax.broadcasted_iota(jnp.int32, (K, K), 1)
     eye = jnp.where(row == col, 1.0, 0.0).astype(F32)
-    rest = jnp.stack([jnp.concatenate([g, eye], axis=1) for g in grams])
-    done = []
-    for p in range(8):
-        panel = rest[:, :8]
-        rest = rest[:, 8:]
-        left = 56 - 8 * p
-        lanes = [8 * p + c for c in range(8)]
-        cols = [jnp.broadcast_to(panel[:, :, c : c + 1], (count, 8, 128)) for c in lanes]
-        below = [jnp.broadcast_to(rest[:, :, c : c + 1], (count, left, 128)) for c in lanes] if left else []
-        out = jnp.zeros((count, 8, 128), F32)
-        for k in range(8):
-            here = sub == k
-            pivot_row = jnp.broadcast_to(panel[:, k : k + 1, :], (count, 8, 128))
-            heads = [jnp.broadcast_to(c[:, k : k + 1, :], (count, 8, 128)) for c in cols[k:]]
-            out = jnp.where(here, pivot_row * lax.rsqrt(heads[0]), out)
-            scale = jnp.where(here, -1.0, cols[k]) * (1.0 / heads[0])
-            panel = jnp.where(here, 0.0, panel) - scale * pivot_row
-            for c in range(k + 1, 8):
-                cols[c] = jnp.where(here, 0.0, cols[c]) - scale * heads[c - k]
-        done.append(out)
-        for k in range(8 if left else 0):
-            rest = rest - below[k] * jnp.broadcast_to(panel[:, k : k + 1, :], (count, left, 128))
-        if hook is not None:
-            hook(p)
+    rests = [jnp.concatenate([g, eye], axis=1) for g in grams]
+    dones = [[] for _ in grams]
+
+    def spread_row(value, k):
+        return jnp.broadcast_to(value[k : k + 1, :], full)
+
+    for p in range(K // WIDE):
+        states = []
+        for rest in rests:
+            panel = rest[:WIDE]
+            cols = [jnp.broadcast_to(panel[:, c : c + 1], full) for c in range(WIDE * p, WIDE * p + WIDE)]
+            states.append([panel, cols, jnp.zeros(full, F32)])
+        for k in range(0, WIDE, 2):
+            here, below = sub == k, sub == k + 1
+            both = here | below
+            for state in states:
+                panel, cols, out = state
+                row0, row1 = spread_row(panel, k), spread_row(panel, k + 1)
+                tops = [spread_row(c, k) for c in cols[k:]]
+                nexts = [spread_row(c, k + 1) for c in cols[k:]]
+                inv0 = 1.0 / tops[0]
+                down, right = nexts[0] * inv0, tops[1] * inv0
+                pivot1 = nexts[1] - down * tops[1]
+                inv1 = 1.0 / pivot1
+                first = jnp.where(here, -1.0, jnp.where(below, 0.0, cols[k]))
+                second = jnp.where(below, -1.0, jnp.where(here, 0.0, cols[k + 1]))
+                scale0 = first * inv0
+                scale1 = (second - right * first) * inv1
+                reduced = row1 - down * row0
+                state[2] = jnp.where(here, row0 * lax.rsqrt(tops[0]), jnp.where(below, reduced * lax.rsqrt(pivot1), out))
+                state[0] = (jnp.where(both, 0.0, panel) - scale0 * row0) - scale1 * reduced
+                for c in range(k + 2, WIDE):
+                    rest_col = nexts[c - k] - down * tops[c - k]
+                    cols[c] = (jnp.where(both, 0.0, cols[c]) - scale0 * tops[c - k]) - scale1 * rest_col
+            if hook is not None:
+                hook((p * WIDE + k) // 2)
+        for n, (panel, _, out) in enumerate(states):
+            dones[n].append(out)
+            tail = rests[n][WIDE:]
+            height = tail.shape[0]
+            if height:
+                terms = [
+                    jnp.broadcast_to(tail[:, c : c + 1], (height, 128)) * jnp.broadcast_to(panel[k : k + 1, :], (height, 128))
+                    for k, c in enumerate(range(WIDE * p, WIDE * p + WIDE))
+                ]
+                while len(terms) > 1:
+                    terms = [x + y for x, y in zip(terms[0::2], terms[1::2])]
+                rests[n] = tail - terms[0]
     keep = lax.broadcasted_iota(jnp.int32, (K, 128), 1) >= lax.broadcasted_iota(jnp.int32, (K, 128), 0)
-    return [jnp.where(keep, jnp.concatenate([d[n] for d in done], axis=0), 0.0) for n in range(count)]
+    return [jnp.where(keep, jnp.concatenate(done, axis=0), 0.0) for done in dones]
 
 
 def kernel(doms, leaves, child_hbm, transfer, toptr, coup, rows_hbm, cols_hbm,
@@ -197,30 +229,46 @@
     pairs = (2 * REACH + 1) * half
     window = []
 
+    def send_window(slot, s, first, count):
+        part = pl.ds(first, count)
+        copy = send(win.at[REACH, part], win.at[REACH - s, part], ws.at[slot], wr.at[slot], (near(s), dom))
+        window.append((copy, REACH - s, first, count))
+
+    sends = [
+        [(2, 0, half), (-2, 0, half)],
+        [(1, 0, half), (-1, 0, half), (3, 0, half // 2), (-3, 0, half // 2)],
+        [(3, half // 2, half // 2), (-3, half // 2, half // 2)],
+    ]
+
+    def send_windows(step):
+        for what in sends[step]:
+            send_window(len(window), *what)
+
     def prepare():
         for load in index_loads:
             load.wait()
         for arrival in gather:
             arrival.wait_recv()
-        for j, s in enumerate(steps):
-            window.append(send(win.at[REACH], win.at[REACH - s], ws.at[j], wr.at[j], (near(s), dom)))
+        send_windows(0)
         run(expand_rows, 0, half, 2)
 
-    def widen():
-        for copy in window:
+    def widen(first, past):
+        for copy, _, _, _ in window[first:past]:
             copy.wait_recv()
-        run(expand_cols, 0, pairs, 4)
+        for _, s, begin, count in window[first:past]:
+            run(expand_cols, s * half + begin, s * half + begin + count, 4)
 
     queues = {"turn": iter(range(K)), "row": iter(range(128)), "col": iter(range(128))}
     bodies = {"turn": turn, "row": row_side, "col": col_side}
 
-    def hook(kind, count):
-        def emit(_):
-            for _ in range(count):
+    def hook(kind, total):
+        def emit(point):
+            points = K // 2
+            for _ in range(total * (point + 1) // points - total * point // points):
                 n = next(queues[kind], None)
                 if n is not None:
                     bodies[kind](n, 0)
-        return emit
+        return emit if total else None
 
     def chunk(kind, count, unroll):
         taken = list(itertools.islice(queues[kind], count))
@@ -228,17 +276,24 @@
 
     def fill(stage):
         if stage == 0:
-            chunk("turn", 32, 4)
+            chunk("turn", TURN_FILL, 4)
             prepare()
-        elif stage == stages - 3:
-            chunk("row", 48, 8)
+        if stage == stages - 3:
+            if stage:
+                send_windows(1)
+                chunk("row", ROW_FILL, 8)
+            run(expand_cols, REACH * half, REACH * half + half, 4)
         elif stage == stages - 2:
+            if stages < 4:
+                send_windows(1)
+            send_windows(2)
             chunk("row", None, 8)
-            widen()
+            widen(0, 2)
         elif stage == stages - 1:
-            chunk("col", 48, 8)
-
-    hooks = {0: ("row", 2, 2), stages - 3: ("row", 2, 2), stages - 2: ("col", 2, 2), stages - 1: ("col", 6, 0)}
+            widen(2, len(window))
+            chunk("col", COL_FILL, 8)
+
+    hooks = {0: ("row", ROW_HOOK, ROW_HOOK), stages - 3: ("row", ROW_HOOK, ROW_HOOK), stages - 1: ("col", COL_HOOK, 128 - COL_FILL - COL_HOOK)}
 
     child_copy.wait()
     stacked = [child[n] for n in range(per)]
@@ -263,7 +318,7 @@
     xa = [product(jnp.where(left, current[2 * s], pltpu.roll(current[2 * s + 1], K, 1)), s) for s in range(own)]
     below = current
     coup_copy.wait()
-    current = factor([dot(x, x, NT) for x in xa], hook("turn", 2))
+    current = factor([dot(x, x, NT) for x in xa], hook("turn", (K - TURN_FILL) // 2))
     x = product(jnp.where(left, current[0], pltpu.roll(current[1], K, 1)), own)
     for n in range(per):
         bottom_out[n] = dot(inverse(below[n]), stacked[n], NN)
@@ -272,7 +327,7 @@
     for s in range(own):
         local_out[own * dom + s] = dot(inverse(current[s]), xa[s], NN)
     arrivals = spread(local_out.at[pl.ds(own * dom, own)], bs, br)
-    (factored,) = factor([dot(x, x, NT)], hook("turn", 2))
+    (factored,) = factor([dot(x, x, NT)], hook("turn", (K - TURN_FILL) // 2))
 
     top_out[0] = jnp.zeros((K, 128), F32)
 
@@ -306,7 +361,8 @@
         xs = [product(jnp.where(left, xr[stage, 2 * s], xr[stage, 2 * s + 1]), 3 * stage + 3 + s) for s in range(2)]
         lowers = factor([dot(v, v, NT) for v in xs], hook(kind, low))
         if stage == stages - 1:
-            stores.append(pltpu.make_async_copy(turned, turned_hbm, out_sem.at[1]))
+            ready = pl.ds(0, (COL_FILL + COL_HOOK) * K)
+            stores.append(pltpu.make_async_copy(turned.at[ready], turned_hbm.at[ready], out_sem.at[1]))
             stores[-1].start()
             for copy in arrivals:
                 copy.wait_recv()
@@ -315,6 +371,10 @@
         x = product(jnp.where(left, lowers[0], pltpu.roll(lowers[1], K, 1)), 3 * stage + 5)
         (factored,) = factor([dot(x, x, NT)], hook(kind, high))
         pending = (stage, lowers, xs, factored, x)
+    if COL_FILL + COL_HOOK < 128:
+        ready = pl.ds((COL_FILL + COL_HOOK) * K, (128 - COL_FILL - COL_HOOK) * K)
+        stores.append(pltpu.make_async_copy(turned.at[ready], turned_hbm.at[ready], out_sem.at[5]))
+        stores[-1].start()
     root_out[...] = factored[:, :K]
     stores.append(pltpu.make_async_copy(root_out, root_hbm, out_sem.at[3]))
     stores[-1].start()
@@ -388,9 +448,9 @@
             pltpu.VMEM(((sides + 1) * nodes, K, 256), BF),
             pltpu.VMEM((stages, 4, K, 128), F32),
             dma((3 * stages + 4,)),
-            dma((5,)),
+            dma((6,)),
             dma((doms - 1,)), dma((doms - 1,)),
-            dma((sides,)), dma((sides,)),
+            dma((8,)), dma((8,)),
             dma((doms - 1,)), dma((doms - 1,)),
             dma((doms - 1,)), dma((doms - 1,)),
             dma((stages, 3)), dma((stages, 3)),

time: 74.6 us -> 67.4 us (0.903)
  the two profiles are of different devices: /device:TPU:2 before, /device:TPU:1 now
where the time goes in v2:
time: 67.4 us; the launch traced here: 67.3 us
  Pallas kernels  66.4 us (99%)
  between operations  0.82 us (1%)
    pallas_call x1, Pallas kernels, on_device(): pl.pallas_call(functools.partial(kernel, doms, leaves), out_shape=small +...  61.2 us
    pallas_call x1, Pallas kernels, on_device(): pl.pallas_call(finish, out_shape=small + (jax.ShapeDtypeStruct((K, K, 256...  5.24 us

profile of v2, /device:TPU:1, one launch (start us, length us, event | category | flops | bytes accessed | tf_op | source)
XLA Modules:
  0.0 67.3 jit_solution(8138145213864222535)
XLA Ops:
  0.6 61.2 %shard_map.101 = (f32[4,64,128]{2,1,0:T(8,128)}, f32[15,64,128]{2,1,0:T(8,128)}, f32[1,64,128]{2,1,0:T(8,128)}, f32[64,64]{1,0:T(8,128)}, f32[8192,128]{1,0:T(8,128)}) custom-call(f32[4,64,128]{2,1,0:T(8,128)} %child_hbm.1, f32[15,64,128]{2,1,0:T(8,128)} %transfer.1, f32[64,64,128]{2,1,0:T(8,128)} %toptr.1, f32[64,64,256]{2,1,0:T(8,128)} %bitcast.3, ...), custom_call_target="tpu_custom_call" | custom-call | tf_op jit(solution)/shard_map/pallas_call | solution.py:433
  61.8 5.2 %shard_map.102 = (f32[4,64,128]{2,1,0:T(8,128)}, f32[15,64,128]{2,1,0:T(8,128)}, f32[1,64,128]{2,1,0:T(8,128)}, f32[64,64]{1,0:T(8,128)}, f32[64,64,256]{2,1,0:T(8,128)}) custom-call(f32[4,64,128]{2,1,0:T(8,128)} %get-tuple-element.15.bottom, f32[15,64,128]{2,1,0:T(8,128)} %get-tuple-element.16.local, f32[1,64,128]{2,1,0:T(8,128)} %get-tuple-element.17.top, ...), custom_call_target="tpu_custom_call" | custom-call | tf_op jit(solution)/shard_map/pallas_call | solution.py:461

commit v3 on v2

--- a/solution.py
+++ b/solution.py
@@ -31,7 +31,6 @@
     return high, (x - high.astype(F32)).astype(BF)
 
 
-WIDE = 16
 TURN_FILL = 32
 ROW_FILL = 48
 ROW_HOOK = 16
@@ -40,6 +39,8 @@
 
 
 def factor(grams, hook=None):
+    double = len(grams) == 1
+    WIDE = 16 if len(grams) < 4 else 8
     full = (WIDE, 128)
     sub = lax.broadcasted_iota(jnp.int32, full, 0)
     row = lax.broadcasted_iota(jnp.int32, (K, K), 0)
@@ -57,11 +58,20 @@
             panel = rest[:WIDE]
             cols = [jnp.broadcast_to(panel[:, c : c + 1], full) for c in range(WIDE * p, WIDE * p + WIDE)]
             states.append([panel, cols, jnp.zeros(full, F32)])
-        for k in range(0, WIDE, 2):
+        for k in range(0, WIDE, 2 if double else 1):
             here, below = sub == k, sub == k + 1
             both = here | below
             for state in states:
                 panel, cols, out = state
+                if not double:
+                    pivot_row = spread_row(panel, k)
+                    heads = [spread_row(c, k) for c in cols[k:]]
+                    state[2] = jnp.where(here, pivot_row * lax.rsqrt(heads[0]), out)
+                    scale = jnp.where(here, -1.0, cols[k]) * (1.0 / heads[0])
+                    state[0] = jnp.where(here, 0.0, panel) - scale * pivot_row
+                    for c in range(k + 1, WIDE):
+                        cols[c] = jnp.where(here, 0.0, cols[c]) - scale * heads[c - k]
+                    continue
                 row0, row1 = spread_row(panel, k), spread_row(panel, k + 1)
                 tops = [spread_row(c, k) for c in cols[k:]]
                 nexts = [spread_row(c, k + 1) for c in cols[k:]]
@@ -79,7 +89,7 @@
                 for c in range(k + 2, WIDE):
                     rest_col = nexts[c - k] - down * tops[c - k]
                     cols[c] = (jnp.where(both, 0.0, cols[c]) - scale0 * tops[c - k]) - scale1 * rest_col
-            if hook is not None:
+            if hook is not None and (double or k % 2):
                 hook((p * WIDE + k) // 2)
         for n, (panel, _, out) in enumerate(states):
             dones[n].append(out)

time: 67.4 us -> 65.2 us (0.967)
  Pallas kernels: 66.4 us -> 64.3 us
    pallas_call x1, Pallas kernels: 61.2 us -> 59 us  [on_device(): pl.pallas_call(functools.partial(kernel, doms, leaves), out_shape=small +...]
where the time goes in v3:
time: 65.2 us; the launch traced here: 65.1 us
  Pallas kernels  64.3 us (99%)
  between operations  0.82 us (1%)
    pallas_call x1, Pallas kernels, on_device(): pl.pallas_call(functools.partial(kernel, doms, leaves), out_shape=small +...  59 us
    pallas_call x1, Pallas kernels, on_device(): pl.pallas_call(finish, out_shape=small + (jax.ShapeDtypeStruct((K, K, 256...  5.24 us

profile of v3, /device:TPU:1, one launch (start us, length us, event | category | flops | bytes accessed | tf_op | source)
XLA Modules:
  0.0 65.1 jit_solution(9849999068993068384)
XLA Ops:
  0.6 59.0 %shard_map.101 = (f32[4,64,128]{2,1,0:T(8,128)}, f32[15,64,128]{2,1,0:T(8,128)}, f32[1,64,128]{2,1,0:T(8,128)}, f32[64,64]{1,0:T(8,128)}, f32[8192,128]{1,0:T(8,128)}) custom-call(f32[4,64,128]{2,1,0:T(8,128)} %child_hbm.1, f32[15,64,128]{2,1,0:T(8,128)} %transfer.1, f32[64,64,128]{2,1,0:T(8,128)} %toptr.1, f32[64,64,256]{2,1,0:T(8,128)} %bitcast.3, ...), custom_call_target="tpu_custom_call" | custom-call | tf_op jit(solution)/shard_map/pallas_call | solution.py:443
  59.7 5.2 %shard_map.102 = (f32[4,64,128]{2,1,0:T(8,128)}, f32[15,64,128]{2,1,0:T(8,128)}, f32[1,64,128]{2,1,0:T(8,128)}, f32[64,64]{1,0:T(8,128)}, f32[64,64,256]{2,1,0:T(8,128)}) custom-call(f32[4,64,128]{2,1,0:T(8,128)} %get-tuple-element.15.bottom, f32[15,64,128]{2,1,0:T(8,128)} %get-tuple-element.16.local, f32[1,64,128]{2,1,0:T(8,128)} %get-tuple-element.17.top, ...), custom_call_target="tpu_custom_call" | custom-call | tf_op jit(solution)/shard_map/pallas_call | solution.py:471

commit v4 on v3

--- a/solution.py
+++ b/solution.py
@@ -333,11 +333,11 @@
     for n in range(per):
         bottom_out[n] = dot(inverse(below[n]), stacked[n], NN)
     stores = [pltpu.make_async_copy(bottom_out, bottom_hbm, out_sem.at[0])]
-    stores[0].start()
     for s in range(own):
         local_out[own * dom + s] = dot(inverse(current[s]), xa[s], NN)
+    (factored,) = factor([dot(x, x, NT)], hook("turn", (K - TURN_FILL) // 2))
+    stores[0].start()
     arrivals = spread(local_out.at[pl.ds(own * dom, own)], bs, br)
-    (factored,) = factor([dot(x, x, NT)], hook("turn", (K - TURN_FILL) // 2))
 
     top_out[0] = jnp.zeros((K, 128), F32)
 

time: 65.2 us -> 67.3 us (1.032)
  Pallas kernels: 64.3 us -> 66.4 us
    pallas_call x1, Pallas kernels: 59 us -> 61.2 us  [on_device(): pl.pallas_call(functools.partial(kernel, doms, leaves), out_shape=small +...]
where the time goes in v4:
time: 67.3 us
  Pallas kernels  66.4 us (99%)
  between operations  0.82 us (1%)
    pallas_call x1, Pallas kernels, on_device(): pl.pallas_call(functools.partial(kernel, doms, leaves), out_shape=small +...  61.2 us
    pallas_call x1, Pallas kernels, on_device(): pl.pallas_call(finish, out_shape=small + (jax.ShapeDtypeStruct((K, K, 256...  5.24 us

profile of v4, /device:TPU:1, one launch (start us, length us, event | category | flops | bytes accessed | tf_op | source)
XLA Modules:
  0.0 67.3 jit_solution(595578237919279257)
XLA Ops:
  0.6 61.2 %shard_map.101 = (f32[4,64,128]{2,1,0:T(8,128)}, f32[15,64,128]{2,1,0:T(8,128)}, f32[1,64,128]{2,1,0:T(8,128)}, f32[64,64]{1,0:T(8,128)}, f32[8192,128]{1,0:T(8,128)}) custom-call(f32[4,64,128]{2,1,0:T(8,128)} %child_hbm.1, f32[15,64,128]{2,1,0:T(8,128)} %transfer.1, f32[64,64,128]{2,1,0:T(8,128)} %toptr.1, f32[64,64,256]{2,1,0:T(8,128)} %bitcast.3, ...), custom_call_target="tpu_custom_call" | custom-call | tf_op jit(solution)/shard_map/pallas_call | solution.py:443
  61.8 5.2 %shard_map.102 = (f32[4,64,128]{2,1,0:T(8,128)}, f32[15,64,128]{2,1,0:T(8,128)}, f32[1,64,128]{2,1,0:T(8,128)}, f32[64,64]{1,0:T(8,128)}, f32[64,64,256]{2,1,0:T(8,128)}) custom-call(f32[4,64,128]{2,1,0:T(8,128)} %get-tuple-element.15.bottom, f32[15,64,128]{2,1,0:T(8,128)} %get-tuple-element.16.local, f32[1,64,128]{2,1,0:T(8,128)} %get-tuple-element.17.top, ...), custom_call_target="tpu_custom_call" | custom-call | tf_op jit(solution)/shard_map/pallas_call | solution.py:471
